TPU v7x, 32 devices: a whole 2x2x4 slice. The times are simulated.
32 devices in a mesh: row: 4 (over y, x), col: 8 (over z, core).
Axes of the slice: x: 2, y: 2, z: 4, core: 2. Of those that a mesh axis runs over, the one named last changes fastest.
Arguments:
- patches: bfloat16 [192, 196, 768], P(('row', 'col')), may hold values from -6 to 6
- shuffle: int32 [192, 196], P(('row', 'col')), may hold values from 0 to 195, each once within a row
- enc_w: float32 [768, 3840], P('row', 'col'), may hold values from -0.21875 to 0.21875
- enc_ffn: float32 [2, 768, 3072], P(None, 'row', 'col'), may hold values from -0.21875 to 0.21875
- dec_proj: float32 [768, 512], P('row', 'col'), may hold values from -0.21875 to 0.21875
- dec_w: float32 [512, 2048], P('row', 'col'), may hold values from -0.25 to 0.25
- dec_ffn: float32 [2, 512, 2048], P(None, 'row', 'col'), may hold values from -0.25 to 0.25
- head_w: float32 [512, 768], replicated, may hold values from -0.25 to 0.25
- smalls: float32 [21248], replicated, may hold values from 0.5 to 1.5
- first_enc_w: float32 [768, 3840], P('row', 'col'), may hold values from -0.00012207031 to 0.00012207031
- first_enc_ffn: float32 [2, 768, 3072], P(None, 'row', 'col'), may hold values from -0.00012207031 to 0.00012207031
- first_dec_proj: float32 [768, 512], P('row', 'col'), may hold values from -0.00012207031 to 0.00012207031
- first_dec_w: float32 [512, 2048], P('row', 'col'), may hold values from -0.00012207031 to 0.00012207031
- first_dec_ffn: float32 [2, 512, 2048], P(None, 'row', 'col'), may hold values from -0.00012207031 to 0.00012207031
- first_head_w: float32 [512, 768], replicated, may hold values from -0.00012207031 to 0.00012207031
- first_smalls: float32 [21248], replicated, may hold values from -0.0014648438 to 0.0014648438
- second_enc_w: float32 [768, 3840], P('row', 'col'), may hold values from 5.406317e-10 to 2.1625268e-09
- second_enc_ffn: float32 [2, 768, 3072], P(None, 'row', 'col'), may hold values from 5.406317e-10 to 2.1625268e-09
- second_dec_proj: float32 [768, 512], P('row', 'col'), may hold values from 5.406317e-10 to 2.1625268e-09
- second_dec_w: float32 [512, 2048], P('row', 'col'), may hold values from 5.406317e-10 to 2.1625268e-09
- second_dec_ffn: float32 [2, 512, 2048], P(None, 'row', 'col'), may hold values from 5.406317e-10 to 2.1625268e-09
- second_head_w: float32 [512, 768], replicated, may hold values from 5.406317e-10 to 2.1625268e-09
- second_smalls: float32 [21248], replicated, may hold values from 5.4063168e-08 to 2.1625267e-07
Outputs:
- new_enc_w: float32 [768, 3840], P('row', 'col')
- new_enc_ffn: float32 [2, 768, 3072], P(None, 'row', 'col')
- new_dec_proj: float32 [768, 512], P('row', 'col')
- new_dec_w: float32 [512, 2048], P('row', 'col')
- new_dec_ffn: float32 [2, 512, 2048], P(None, 'row', 'col')
- new_head_w: float32 [512, 768], replicated
- new_smalls: float32 [21248], replicated
- moment_enc_w: float32 [768, 3840], P('row', 'col')
- moment_enc_ffn: float32 [2, 768, 3072], P(None, 'row', 'col')
- moment_dec_proj: float32 [768, 512], P('row', 'col')
- moment_dec_w: float32 [512, 2048], P('row', 'col')
- moment_dec_ffn: float32 [2, 512, 2048], P(None, 'row', 'col')
- moment_head_w: float32 [512, 768], replicated
- moment_smalls: float32 [21248], replicated
- square_enc_w: float32 [768, 3840], P('row', 'col')
- square_enc_ffn: float32 [2, 768, 3072], P(None, 'row', 'col')
- square_dec_proj: float32 [768, 512], P('row', 'col')
- square_dec_w: float32 [512, 2048], P('row', 'col')
- square_dec_ffn: float32 [2, 512, 2048], P(None, 'row', 'col')
- square_head_w: float32 [512, 768], replicated
- square_smalls: float32 [21248], replicated
- loss: float32 [], replicated
Inputs may be any that keep to these rules, and one draw needn't show every extreme that they name: `shuffle`: each image's row names every patch index once.
All inputs are finite; a program needn't handle non-finite values.
Results may differ from a plain program's by a relative error of at most 0.00095.
The roundings to bfloat16 on the way count: a program that leaves them out, or rounds other values in their place, can miss the bound.
Values may be sent and summed in bfloat16 or wider, within the bound.
A program may use at most 256 MiB of HBM per device.

v0:
```python
import math

import jax
import jax.numpy as jnp
from jax import lax
from jax.sharding import PartitionSpec as P

D = 768
HE = 12
F = 3072
E = 512
HD = 16
H = 2048
P_SIZE = 768
SIDE = 14
KEEP = 49
STEP = 5
PATCHES = 196


norm_eps = 1e-06
low_type = jnp.bfloat16
high_type = jnp.float32


def product_of(left, right):
    return jnp.dot(left, right, preferred_element_type=high_type)


def against_rows(left, right):
    return lax.dot_general(left, right, (((1,), (1,)), ((), ())), preferred_element_type=high_type)


def weight_grad(left, right):
    return lax.dot_general(left, right, (((0,), (0,)), ((), ())), preferred_element_type=high_type)


def layer_norm(rows, gain, shift):
    mean = jnp.mean(rows, -1, keepdims=True)
    centred = rows - mean
    spread = jnp.mean(centred * centred, -1, keepdims=True)
    return centred * lax.rsqrt(spread + norm_eps) * gain + shift


def norm_back(rows, gain, shift, grad):
    return jax.vjp(layer_norm, rows, gain, shift)[1](grad)


def gelu_exact(inputs):
    return jax.nn.gelu(inputs, approximate=False)


def sincos_table(width):
    quarter = width // 4
    omega = 1.0 / 10000.0 ** (jnp.arange(quarter).astype(high_type) / quarter)
    coord = jnp.arange(SIDE * SIDE)

    def half(place):
        angle = place.astype(high_type)[:, None] * omega[None, :]
        return jnp.concatenate([jnp.sin(angle), jnp.cos(angle)], 1)

    return jnp.concatenate([half(coord // SIDE), half(coord % SIDE)], 1)


def unpack(smalls):
    first = 12 * D
    second = first + F
    third = second + 12 * E
    fourth = third + H
    return (
        smalls[:first].reshape(12, D),
        smalls[first:second],
        smalls[second:third].reshape(12, E),
        smalls[third:fourth],
        smalls[fourth:],
    )


def split_heads(tensor, batch, heads):
    return tensor.reshape(batch, tensor.shape[0] // batch, heads, tensor.shape[1] // heads)


def column_sums(tensor):
    return jnp.sum(tensor.astype(high_type), 0)


def layer_forward(hidden, wide, ffn_w, vectors, bias_up, heads, batch):
    width = hidden.shape[1]
    scale = 1.0 / math.sqrt(width // heads)
    normed = layer_norm(hidden, vectors[2], vectors[3]).astype(low_type)
    projected = product_of(normed, wide[:, : 3 * width])
    query_rows = ((projected[:, :width] + vectors[4]) * scale).astype(low_type)
    key_rows = projected[:, width : 2 * width].astype(low_type)
    value_rows = (projected[:, 2 * width :] + vectors[5]).astype(low_type)
    scores = jnp.einsum(
        "bqhd,bkhd->bhqk",
        split_heads(query_rows, batch, heads),
        split_heads(key_rows, batch, heads),
        preferred_element_type=high_type,
    )
    row_max = jnp.max(scores, -1, keepdims=True)
    raised = jnp.exp(scores - row_max)
    total = jnp.sum(raised, -1, keepdims=True)
    log_total = row_max + jnp.log(total)
    attention = (raised / total).astype(low_type)
    mixed = (
        jnp.einsum(
            "bhqk,bkhd->bqhd",
            attention,
            split_heads(value_rows, batch, heads),
            preferred_element_type=high_type,
        )
        .reshape(hidden.shape)
        .astype(low_type)
    )
    middle = hidden + (product_of(mixed, wide[:, 3 * width :]) + vectors[6])
    normed_two = layer_norm(middle, vectors[7], vectors[8]).astype(low_type)
    up_out = product_of(normed_two, ffn_w[0]) + bias_up
    active = gelu_exact(up_out).astype(low_type)
    down = against_rows(active, ffn_w[1])
    output = middle + (down + vectors[9])
    saved = (
        hidden,
        normed,
        query_rows,
        key_rows,
        value_rows,
        log_total,
        mixed,
        middle,
        normed_two,
        up_out,
        active,
    )
    return (output, saved)


def layer_backward(grad_out, saved, wide, ffn_w, vectors, heads, batch):
    (
        hidden,
        normed,
        query_rows,
        key_rows,
        value_rows,
        log_total,
        mixed,
        middle,
        source,
        up_out,
        active,
    ) = saved
    width = hidden.shape[1]
    scale = 1.0 / math.sqrt(width // heads)
    grad_down = grad_out.astype(low_type)
    grad_active = product_of(grad_down, ffn_w[1])
    grad_w_down = weight_grad(grad_down, active)
    grad_up = jax.vjp(gelu_exact, up_out)[1](grad_active)[0].astype(low_type)
    grad_w_up = weight_grad(source, grad_up)
    grad_normed_two = against_rows(grad_up, ffn_w[0])
    grad_middle, gain_two, shift_two = norm_back(middle, vectors[7], vectors[8], grad_normed_two)
    grad_middle = grad_middle + grad_out
    grad_branch = grad_middle.astype(low_type)
    grad_w_out = weight_grad(mixed, grad_branch)
    grad_mixed = split_heads(
        against_rows(grad_branch, wide[:, 3 * width :]).astype(low_type), batch, heads
    )
    query_heads = split_heads(query_rows, batch, heads)
    key_heads = split_heads(key_rows, batch, heads)
    value_heads = split_heads(value_rows, batch, heads)
    scores = jnp.einsum("bqhd,bkhd->bhqk", query_heads, key_heads, preferred_element_type=high_type)
    attention = jnp.exp(scores - log_total)
    grad_values = jnp.einsum(
        "bhqk,bqhd->bkhd", attention.astype(low_type), grad_mixed, preferred_element_type=high_type
    )
    grad_attention = jnp.einsum(
        "bqhd,bkhd->bhqk", grad_mixed, value_heads, preferred_element_type=high_type
    )
    grad_scores = (
        attention * (grad_attention - jnp.sum(grad_attention * attention, -1, keepdims=True))
    ).astype(low_type)
    grad_query = (
        jnp.einsum("bhqk,bkhd->bqhd", grad_scores, key_heads, preferred_element_type=high_type)
        * scale
    )
    grad_keys = jnp.einsum(
        "bhqk,bqhd->bkhd", grad_scores, query_heads, preferred_element_type=high_type
    )
    grad_projected = jnp.concatenate(
        [
            grad_query.reshape(hidden.shape),
            grad_keys.reshape(hidden.shape),
            grad_values.reshape(hidden.shape),
        ],
        1,
    ).astype(low_type)
    grad_w_in = weight_grad(normed, grad_projected)
    grad_normed = against_rows(grad_projected, wide[:, : 3 * width])
    grad_hidden, gain_one, shift_one = norm_back(hidden, vectors[2], vectors[3], grad_normed)
    sums = column_sums(grad_projected)
    zero_row = jnp.zeros((width,), high_type)
    grad_vectors = jnp.stack(
        [
            zero_row,
            zero_row,
            gain_one,
            shift_one,
            sums[:width],
            sums[2 * width :],
            column_sums(grad_branch),
            gain_two,
            shift_two,
            column_sums(grad_down),
            zero_row,
            zero_row,
        ]
    )
    grad_wide = jnp.concatenate([grad_w_in, grad_w_out], 1)
    return (
        grad_hidden + grad_middle,
        grad_wide,
        jnp.stack([grad_w_up, grad_w_down]),
        grad_vectors,
        column_sums(grad_up),
    )


def adam_update(weight, grad, first, second, bias_one, bias_two, decay):
    first_new = 0.5 * first + 0.5 * grad
    second_new = 0.5 * second + 0.5 * grad * grad
    direction = first_new / bias_one / (jnp.sqrt(second_new / bias_two) + 1e-08)
    return (weight - 0.02 * (direction + decay * weight), first_new, second_new)


def body(
    patches,
    shuffle,
    enc_w,
    enc_ffn,
    dec_proj,
    dec_w,
    dec_ffn,
    head_w,
    smalls,
    first_enc_w,
    first_enc_ffn,
    first_dec_proj,
    first_dec_w,
    first_dec_ffn,
    first_head_w,
    first_smalls,
    second_enc_w,
    second_enc_ffn,
    second_dec_proj,
    second_dec_w,
    second_dec_ffn,
    second_head_w,
    second_smalls,
):
    rowed = (
        lax.all_gather(enc_w.astype(low_type), "row", axis=0, tiled=True),
        lax.all_gather(enc_ffn.astype(low_type), "row", axis=1, tiled=True),
        lax.all_gather(dec_proj.astype(low_type), "row", axis=0, tiled=True),
        lax.all_gather(dec_w.astype(low_type), "row", axis=0, tiled=True),
        lax.all_gather(dec_ffn.astype(low_type), "row", axis=1, tiled=True),
    )
    enc_full, enc_ffn_w, proj_full, dec_full, dec_ffn_w = (
        lax.all_gather(rowed[0], "col", axis=1, tiled=True),
        lax.all_gather(rowed[1], "col", axis=2, tiled=True),
        lax.all_gather(rowed[2], "col", axis=1, tiled=True),
        lax.all_gather(rowed[3], "col", axis=1, tiled=True),
        lax.all_gather(rowed[4], "col", axis=2, tiled=True),
    )
    head_low = head_w.astype(low_type)
    enc_vec, enc_up, dec_vec, dec_up, head_bias = unpack(smalls)
    batch = patches.shape[0]
    picks = shuffle[:, :KEEP, None] == jnp.arange(PATCHES)[None, None, :]
    pick_float = picks.astype(high_type)
    masked = 1.0 - jnp.sum(pick_float, 1)
    kept = (
        jnp.einsum(
            "bjp,bpc->bjc", picks.astype(low_type), patches, preferred_element_type=high_type
        )
        .astype(low_type)
        .reshape(batch * KEEP, P_SIZE)
    )
    embed = (product_of(kept, enc_full[:, :D]) + enc_vec[0]).reshape(batch, KEEP, D)
    embed = embed + jnp.einsum(
        "bjp,pc->bjc", pick_float, sincos_table(D), precision=lax.Precision.HIGHEST
    )
    start_rows = jnp.concatenate([jnp.broadcast_to(enc_vec[1], (batch, 1, D)), embed], 1).reshape(
        batch * (KEEP + 1), D
    )
    enc_out, enc_saved = layer_forward(
        start_rows, enc_full[:, D:], enc_ffn_w, enc_vec, enc_up, HE, batch
    )
    latent = layer_norm(enc_out, enc_vec[10], enc_vec[11]).astype(low_type)
    entry = (product_of(latent, proj_full) + dec_vec[0]).reshape(batch, KEEP + 1, E)
    placed = (
        jnp.einsum("bjp,bjc->bpc", pick_float, entry[:, 1:], precision=lax.Precision.HIGHEST)
        + masked[:, :, None] * dec_vec[1]
        + sincos_table(E)
    )
    dec_rows = jnp.concatenate([entry[:, :1], placed], 1).reshape(batch * (PATCHES + 1), E)
    dec_out, dec_saved = layer_forward(dec_rows, dec_full, dec_ffn_w, dec_vec, dec_up, HD, batch)
    patch_rows = dec_out.reshape(batch, PATCHES + 1, E)[:, 1:].reshape(batch * PATCHES, E)
    final = layer_norm(patch_rows, dec_vec[10], dec_vec[11]).astype(low_type)
    predict = product_of(final, head_low) + head_bias
    pixels = patches.astype(high_type).reshape(batch * PATCHES, P_SIZE)
    centred = pixels - jnp.mean(pixels, -1, keepdims=True)
    target = centred * lax.rsqrt(jnp.mean(centred * centred, -1, keepdims=True) + norm_eps)
    weight_mask = masked.reshape(batch * PATCHES, 1)
    error = predict - target
    loss_local = jnp.sum(weight_mask * error * error)
    count = batch * lax.axis_size("row") * lax.axis_size("col") * (PATCHES - KEEP) * P_SIZE
    grad_predict = (2.0 * weight_mask * error / count).astype(low_type)
    grad_head = weight_grad(final, grad_predict)
    grad_final = against_rows(grad_predict, head_low)
    grad_patch_rows, dec_gain, dec_shift = norm_back(
        patch_rows, dec_vec[10], dec_vec[11], grad_final
    )
    grad_dec_out = jnp.concatenate(
        [jnp.zeros((batch, 1, E), high_type), grad_patch_rows.reshape(batch, PATCHES, E)], 1
    ).reshape(batch * (PATCHES + 1), E)
    grad_dec_rows, grad_dec_wide, grad_dec_ffn, grad_dec_vec, grad_dec_up = layer_backward(
        grad_dec_out, dec_saved, dec_full, dec_ffn_w, dec_vec, HD, batch
    )
    grad_placed = grad_dec_rows.reshape(batch, PATCHES + 1, E)
    grad_mask_token = jnp.sum(masked[:, :, None] * grad_placed[:, 1:], (0, 1))
    grad_entry = jnp.concatenate(
        [
            grad_placed[:, :1],
            jnp.einsum(
                "bjp,bpc->bjc", pick_float, grad_placed[:, 1:], precision=lax.Precision.HIGHEST
            ),
        ],
        1,
    )
    grad_entry = grad_entry.reshape(batch * (KEEP + 1), E).astype(low_type)
    grad_proj = weight_grad(latent, grad_entry)
    grad_latent = against_rows(grad_entry, proj_full)
    grad_enc_out, enc_gain, enc_shift = norm_back(enc_out, enc_vec[10], enc_vec[11], grad_latent)
    grad_start, grad_enc_wide, grad_enc_ffn, grad_enc_vec, grad_enc_up = layer_backward(
        grad_enc_out, enc_saved, enc_full[:, D:], enc_ffn_w, enc_vec, HE, batch
    )
    grad_start = grad_start.reshape(batch, KEEP + 1, D)
    grad_embed = grad_start[:, 1:].reshape(batch * KEEP, D).astype(low_type)
    grad_patch = weight_grad(kept, grad_embed)
    enc_extra = (
        jnp.zeros((12, D), high_type)
        .at[0]
        .set(column_sums(grad_embed))
        .at[1]
        .set(jnp.sum(grad_start[:, 0], 0))
        .at[10]
        .set(enc_gain)
        .at[11]
        .set(enc_shift)
    )
    dec_extra = (
        jnp.zeros((12, E), high_type)
        .at[0]
        .set(column_sums(grad_entry))
        .at[1]
        .set(grad_mask_token)
        .at[10]
        .set(dec_gain)
        .at[11]
        .set(dec_shift)
    )
    grad_smalls = jnp.concatenate(
        [
            (grad_enc_vec + enc_extra).reshape(-1),
            grad_enc_up,
            (grad_dec_vec + dec_extra).reshape(-1),
            grad_dec_up,
            column_sums(grad_predict),
        ]
    )
    grad_enc_full = jnp.concatenate([grad_patch, grad_enc_wide], 1)
    col_enc, col_enc_ffn, col_proj, col_dec, col_dec_ffn = (
        lax.psum_scatter(grad_enc_full, "col", scatter_dimension=1, tiled=True),
        lax.psum_scatter(grad_enc_ffn, "col", scatter_dimension=2, tiled=True),
        lax.psum_scatter(grad_proj, "col", scatter_dimension=1, tiled=True),
        lax.psum_scatter(grad_dec_wide, "col", scatter_dimension=1, tiled=True),
        lax.psum_scatter(grad_dec_ffn, "col", scatter_dimension=2, tiled=True),
    )
    sharded = (
        lax.psum_scatter(col_enc, "row", scatter_dimension=0, tiled=True),
        lax.psum_scatter(col_enc_ffn, "row", scatter_dimension=1, tiled=True),
        lax.psum_scatter(col_proj, "row", scatter_dimension=0, tiled=True),
        lax.psum_scatter(col_dec, "row", scatter_dimension=0, tiled=True),
        lax.psum_scatter(col_dec_ffn, "row", scatter_dimension=1, tiled=True),
    )
    summed_head, summed_smalls, loss_sum = lax.psum(
        (grad_head, grad_smalls, loss_local), ("row", "col")
    )
    grads = (sharded[0], sharded[1], sharded[2], sharded[3], sharded[4], summed_head, summed_smalls)
    params = (enc_w, enc_ffn, dec_proj, dec_w, dec_ffn, head_w, smalls)
    firsts = (
        first_enc_w,
        first_enc_ffn,
        first_dec_proj,
        first_dec_w,
        first_dec_ffn,
        first_head_w,
        first_smalls,
    )
    seconds = (
        second_enc_w,
        second_enc_ffn,
        second_dec_proj,
        second_dec_w,
        second_dec_ffn,
        second_head_w,
        second_smalls,
    )
    decays = (0.05, 0.05, 0.05, 0.05, 0.05, 0.05, 0.0)
    bias_one = 1.0 - 0.5**STEP
    bias_two = 1.0 - 0.5**STEP
    results = [
        adam_update(
            params[index],
            grads[index],
            firsts[index],
            seconds[index],
            bias_one,
            bias_two,
            decays[index],
        )
        for index in range(7)
    ]
    news = [item[0] for item in results]
    moments = [item[1] for item in results]
    squares = [item[2] for item in results]
    return (
        news[0],
        news[1],
        news[2],
        news[3],
        news[4],
        news[5],
        news[6],
        moments[0],
        moments[1],
        moments[2],
        moments[3],
        moments[4],
        moments[5],
        moments[6],
        squares[0],
        squares[1],
        squares[2],
        squares[3],
        squares[4],
        squares[5],
        squares[6],
        loss_sum / count,
    )


def solution(mesh):
    in_specs = (
        P(("row", "col"), None, None),
        P(("row", "col"), None),
        P("row", "col"),
        P(None, "row", "col"),
        P("row", "col"),
        P("row", "col"),
        P(None, "row", "col"),
        P(),
        P(),
        P("row", "col"),
        P(None, "row", "col"),
        P("row", "col"),
        P("row", "col"),
        P(None, "row", "col"),
        P(),
        P(),
        P("row", "col"),
        P(None, "row", "col"),
        P("row", "col"),
        P("row", "col"),
        P(None, "row", "col"),
        P(),
        P(),
    )
    out_specs = (
        P("row", "col"),
        P(None, "row", "col"),
        P("row", "col"),
        P("row", "col"),
        P(None, "row", "col"),
        P(),
        P(),
        P("row", "col"),
        P(None, "row", "col"),
        P("row", "col"),
        P("row", "col"),
        P(None, "row", "col"),
        P(),
        P(),
        P("row", "col"),
        P(None, "row", "col"),
        P("row", "col"),
        P("row", "col"),
        P(None, "row", "col"),
        P(),
        P(),
        P(),
    )
    return jax.shard_map(body, mesh=mesh, in_specs=in_specs, out_specs=out_specs, check_vma=False)
```

profile of v0, /device:TPU:0, one launch (start us, length us, event | category | flops | bytes accessed | tf_op | source)
XLA Modules:
  0.0 1290.7 jit_solution(14339462323215562104)
XLA Ops:
  10.2 13.5 %all_gather.30 = bf16[768,480]{1,0:T(8,128)(2,1)S(1)} all-gather(bf16[192,480]{1,0:T(8,128)(2,1)S(1)} %convert_element_type.238), channel_id=1, replica_groups=mesh['row'=4,'col'=8] {'row'}, dimensions={0}, use_global_device_ids=true | all-gather | bytes 921600 | tf_op jit(solution)/shard_map/all_gather | solution.py:260
  24.9 16.0 %all-gather.9.cloned.1.call-done = bf16[2,768,384]{2,1,0:T(8,128)(2,1)} async-done(((bf16[2,192,384]{2,1,0:T(8,128)(2,1)}), bf16[2,768,384]{2,1,0:T(8,128)(2,1)}) %all-gather.9.cloned.1.call-update) | async-done | bytes 1179664 | tf_op jit(solution)/shard_map/all_gather | solution.py:261
  50.7 10.6 all_gather.38
  77.5 20.9 %all_gather.35 = bf16[768,512]{0,1:T(8,128)(2,1)} all-gather(bf16[768,64]{0,1:T(8,128)(2,1)S(1)} %reshape.803), channel_id=1, replica_groups=mesh['row'=4,'col'=8] {'col'}, dimensions={1}, use_global_device_ids=true | all-gather | bytes 884736 | tf_op jit(solution)/shard_map/all_gather | solution.py:269
  129.9 71.9 %all-gather.11.cloned.1.call-done = bf16[2,768,3072]{2,1,0:T(8,128)(2,1)} async-done(((bf16[2,768,384]{2,1,0:T(8,128)(2,1)}), bf16[2,768,3072]{2,1,0:T(8,128)(2,1)}) %all-gather.11.cloned.1.call-update) | async-done | bytes 9437200 | tf_op jit(solution)/shard_map/all_gather | solution.py:268
  201.9 13.0 %multiply_convert_fusion.2 = (bf16[300,3072]{1,0:T(8,128)(2,1)S(1)}, f32[300,3072]{1,0:T(8,128)}, f32[300,3072]{1,0:T(8,128)}) fusion(f32[3072]{0:T(1024)S(1)} %slice-done.1, bf16[2,768,3072]{2,1,0:T(8,128)(2,1)} %all-gather.11.cloned.1.call-done, f32[300,768]{1,0:T(8,128)S(1)} %get-tuple-element.240, f32[768]{0:T(1024)S(1)} %get-tuple-element.211, ...), kind=kOutput, calls=%fused_computation.50 | convolution fusion | flops 1477555200 | bytes 14877024 | tf_op jit(solution)/shard_map/dot_general | solution.py:27
  255.9 11.1 fusion.154
  267.0 11.6 fusion
  295.1 27.0 %multiply_convert_fusion.1 = (bf16[1182,2048]{1,0:T(8,128)(2,1)S(1)}, f32[1182,2048]{1,0:T(8,128)}, f32[1182,2048]{1,0:T(8,128)}) fusion(f32[2048]{0:T(1024)S(1)} %slice-done, bf16[2,512,2048]{2,1,0:T(8,128)(2,1)} %all-gather.15.cloned.1.call-done, f32[1182,512]{1,0:T(8,128)S(1)} %get-tuple-element.247, f32[512]{0:T(512)S(1)} %get-tuple-element.199, ...), kind=kOutput, calls=%fused_computation.16 | convolution fusion | flops 2641628160 | bytes 28746992 | tf_op jit(solution)/shard_map/dot_general | solution.py:27
  362.6 12.6 convert_reduce_fusion
  399.3 11.4 fusion.47
  410.7 14.9 %multiply_reduce_fusion = (f32[6,16,197]{2,1,0:T(8,128)S(1)}, f32[6,16,197,197]{2,3,1,0:T(8,128)}) fusion(f32[6,16,197,197]{2,3,1,0:T(8,128)} %get-tuple-element.245, f32[6,16,197]{2,1,0:T(8,128)S(1)} %log_add_fusion, bf16[6,197,16,32]{1,0,3,2:T(8,128)(2,1)} %reshape.768, bf16[6,197,16,32]{1,0,3,2:T(8,128)(2,1)} %reshape.774), kind=kOutput, calls=%fused_computation.1 | convolution fusion | flops 249600576 | bytes 32377344 | tf_op jit(solution)/shard_map/bqhd,bkhd->bhqk/dot_general | solution.py:175
  425.6 13.7 %multiply_convert_fusion = bf16[6,16,197,197]{2,3,1,0:T(8,128)(2,1)S(1)} fusion(f32[6,16,197,197]{2,3,1,0:T(8,128)} %get-tuple-element.252, f32[6,16,197,197]{2,3,1,0:T(8,128)} %get-tuple-element.245, f32[6,16,197]{2,1,0:T(8,128)S(1)} %get-tuple-element.251, f32[6,16,197]{2,1,0:T(8,128)S(1)} %log_add_fusion), kind=kLoop, calls=%fused_computation | loop fusion | flops 14902656 | bytes 37407936 | tf_op jit(solution)/shard_map/convert_element_type | solution.py:180
  576.7 12.4 copy.196
  627.4 43.8 %reduce-scatter.27.cloned.1.call-done = f32[2,512,256]{2,1,0:T(8,128)} async-done(((f32[2,512,2048]{2,1,0:T(8,128)}), f32[2,512,256]{2,1,0:T(8,128)}) %reduce-scatter.27.cloned.1.call-update) | async-done | bytes 1048592 | tf_op jit(solution)/shard_map/reduce_scatter | solution.py:385
  671.3 122.4 %reduce-scatter.31.cloned.1.call-done = f32[480,768]{1,0:T(8,128)} async-done(((f32[3840,768]{1,0:T(8,128)}), f32[480,768]{1,0:T(8,128)}) %reduce-scatter.31.cloned.1.call-update) | async-done | bytes 1474576
  796.8 185.5 %reduce-scatter.17.cloned.1.call-done = f32[2,768,384]{2,1,0:T(8,128)} async-done(((f32[2,768,3072]{2,1,0:T(8,128)}), f32[2,768,384]{2,1,0:T(8,128)}) %reduce-scatter.17.cloned.1.call-update) | async-done | bytes 2359312 | tf_op jit(solution)/shard_map/reduce_scatter | solution.py:382
  982.3 38.4 %psum.23 = f32[]{:T(128)} all-reduce(f32[]{:T(128)} %get-tuple-element.189), channel_id=1, replica_groups=mesh['row'=4,'col'=8] {'row','col'}, use_global_device_ids=true, to_apply=%region_71.72 | all-reduce | flops 1 | bytes 8 | tf_op jit(solution)/shard_map/psum | solution.py:394
  1021.3 98.6 %all-reduce.6.cloned.1.call-done = (f32[512,768]{1,0:T(8,128)}, f32[21248]{0:T(1024)}) async-done(((f32[512,768]{1,0:T(8,128)}, f32[21248]{0:T(1024)}), (f32[512,768]{1,0:T(8,128)}, f32[21248]{0:T(1024)})) %all-reduce.6.cloned.1.call-update) | async-done | bytes 1657872 | tf_op jit(solution)/shard_map/psum | solution.py:394
  1125.7 21.3 %reduce-scatter.33.cloned.1.call-done = f32[192,64]{1,0:T(8,128)} async-done(((f32[768,64]{1,0:T(8,128)}), f32[192,64]{1,0:T(8,128)}) %reduce-scatter.33.cloned.1.call-update) | async-done | bytes 49168
  1149.6 25.3 %reduce-scatter.25.cloned.1.call-done = f32[128,256]{1,0:T(8,128)} async-done(((f32[512,256]{1,0:T(8,128)}), f32[128,256]{1,0:T(8,128)}) %reduce-scatter.25.cloned.1.call-update) | async-done | bytes 131088 | tf_op jit(solution)/shard_map/reduce_scatter | solution.py:391
  1176.7 28.6 %reduce-scatter.29.cloned.1.call-done = f32[2,128,256]{2,1,0:T(8,128)} async-done(((f32[2,512,256]{2,1,0:T(8,128)}), f32[2,128,256]{2,1,0:T(8,128)}) %reduce-scatter.29.cloned.1.call-update) | async-done | bytes 262160 | tf_op jit(solution)/shard_map/reduce_scatter | solution.py:392
  1207.4 32.0 %reduce-scatter.15.cloned.1.call-done = f32[192,480]{1,0:T(8,128)} async-done(((f32[768,480]{1,0:T(8,128)}), f32[192,480]{1,0:T(8,128)}) %reduce-scatter.15.cloned.1.call-update) | async-done | bytes 368656 | tf_op jit(solution)/shard_map/reduce_scatter | solution.py:388
  1241.6 38.4 %reduce-scatter.19.cloned.1.call-done = f32[2,192,384]{2,1,0:T(8,128)} async-done(((f32[2,768,384]{2,1,0:T(8,128)}), f32[2,192,384]{2,1,0:T(8,128)}) %reduce-scatter.19.cloned.1.call-update) | async-done | bytes 589840 | tf_op jit(solution)/shard_map/reduce_scatter | solution.py:389
  (584 shorter events, 377.4 us)
Async XLA Ops:
  7.2 33.7 %all-gather.9.cloned.1.call-start = ((), (), s32[]{:S(2)}) async-start(), calls=%async_computation.11 | async-start | bytes 1474560 | tf_op jit(solution)/shard_map/all_gather | solution.py:261
  9.1 101.7 %all-gather.7.cloned.1.call-start = ((), (), s32[]{:S(2)}) async-start(), calls=%async_computation.10 | async-start | bytes 6635520 | tf_op jit(solution)/shard_map/all_gather | solution.py:267
  24.8 177.0 %all-gather.11.cloned.1.call-start = ((), (), s32[]{:S(2)}) async-start(), calls=%async_computation.12 | async-start | bytes 10616832 | tf_op jit(solution)/shard_map/all_gather | solution.py:268
  40.9 191.7 %all-gather.13.cloned.1.call-start = ((), (), s32[]{:S(2)}) async-start(), calls=%async_computation.13 | async-start | bytes 2359296 | tf_op jit(solution)/shard_map/all_gather | solution.py:270
  50.6 244.4 %all-gather.15.cloned.1.call-start = ((), (), s32[]{:S(2)}) async-start(), calls=%async_computation.14 | async-start | bytes 4718592 | tf_op jit(solution)/shard_map/all_gather | solution.py:271
  61.4 563.4 %reduce-scatter.21.cloned.1.call-start = ((), (), s32[]{:S(2)}) async-start(), calls=%async_computation.18 | async-start | bytes 1769472 | tf_op jit(solution)/shard_map/reduce_scatter | solution.py:383
  63.8 168.9 %copy-start.129 = (f32[512]{0:T(512)}, f32[512]{0:T(512)S(1)}, u32[]{:S(2)}) copy-start(f32[512]{0:T(512)S(1)} %get-tuple-element.205) | copy-start | bytes 6148
  63.8 168.9 %copy-start.133 = (f32[512]{0:T(512)}, f32[512]{0:T(512)S(1)}, u32[]{:S(2)}) copy-start(f32[512]{0:T(512)S(1)} %get-tuple-element.204) | copy-start | bytes 6148
  64.4 152.7 %copy-start.94 = (f32[768]{0:T(1024)}, f32[768]{0:T(1024)S(1)}, u32[]{:S(2)}) copy-start(f32[768]{0:T(1024)S(1)} %get-tuple-element.208) | copy-start | bytes 9220
  64.4 152.7 %copy-start.122 = (f32[768]{0:T(1024)}, f32[768]{0:T(1024)S(1)}, u32[]{:S(2)}) copy-start(f32[768]{0:T(1024)S(1)} %get-tuple-element.209) | copy-start | bytes 9220
  64.4 153.8 %copy-start.78 = (s32[6,49]{1,0:T(8,128)}, s32[6,49]{1,0:T(8,128)S(1)}, u32[]{:S(2)}) copy-start(s32[6,49]{1,0:T(8,128)S(1)} %slice.352) | copy-start | bytes 3532
  67.4 150.9 %copy-start.80 = (f32[6,196]{1,0:T(8,128)}, f32[6,196]{1,0:T(8,128)S(1)}, u32[]{:S(2)}) copy-start(f32[6,196]{1,0:T(8,128)S(1)} %broadcast_subtract_fusion) | copy-start | bytes 14116
  497.6 129.1 %reduce-scatter.23.cloned.1.call-start = ((), (), s32[]{:S(2)}) async-start(), calls=%async_computation.19 | async-start | bytes 4718592 | tf_op jit(solution)/shard_map/reduce_scatter | solution.py:384
  506.7 164.5 %reduce-scatter.27.cloned.1.call-start = ((), (), s32[]{:S(2)}) async-start(), calls=%async_computation.21 | async-start | bytes 9437184 | tf_op jit(solution)/shard_map/reduce_scatter | solution.py:385
  521.4 272.3 %reduce-scatter.31.cloned.1.call-start = ((), (), s32[]{:S(2)}) async-start(), calls=%async_computation.23 | async-start | bytes 13271040
  589.2 393.1 %reduce-scatter.17.cloned.1.call-start = ((), (), s32[]{:S(2)}) async-start(), calls=%async_computation.16 | async-start | bytes 21233664 | tf_op jit(solution)/shard_map/reduce_scatter | solution.py:382
  603.3 516.6 %all-reduce.6.cloned.1.call-start = ((), (), s32[]{:S(2)}) async-start(), calls=%async_computation.25 | async-start | bytes 3317760 | tf_op jit(solution)/shard_map/psum | solution.py:394
  624.7 522.3 %reduce-scatter.33.cloned.1.call-start = ((), (), s32[]{:S(2)}) async-start(), calls=%async_computation.24 | async-start | bytes 491520
  626.6 548.3 %reduce-scatter.25.cloned.1.call-start = ((), (), s32[]{:S(2)}) async-start(), calls=%async_computation.20 | async-start | bytes 655360 | tf_op jit(solution)/shard_map/reduce_scatter | solution.py:391
  627.4 578.0 %reduce-scatter.29.cloned.1.call-start = ((), (), s32[]{:S(2)}) async-start(), calls=%async_computation.22 | async-start | bytes 1310720 | tf_op jit(solution)/shard_map/reduce_scatter | solution.py:392
  671.2 568.2 %reduce-scatter.15.cloned.1.call-start = ((), (), s32[]{:S(2)}) async-start(), calls=%async_computation.15 | async-start | bytes 1966080 | tf_op jit(solution)/shard_map/reduce_scatter | solution.py:388
  796.7 323.2 %copy-start.52 = (f32[512,768]{1,0:T(8,128)S(1)}, f32[512,768]{1,0:T(8,128)}, u32[]{:S(2)}) copy-start(f32[512,768]{1,0:T(8,128)} %param.46) | copy-start | bytes 4718596
  796.7 323.2 %copy-start.53 = (f32[512,768]{1,0:T(8,128)S(1)}, f32[512,768]{1,0:T(8,128)}, u32[]{:S(2)}) copy-start(f32[512,768]{1,0:T(8,128)} %param.53) | copy-start | bytes 4718596
  796.7 483.3 %reduce-scatter.19.cloned.1.call-start = ((), (), s32[]{:S(2)}) async-start(), calls=%async_computation.17 | async-start | bytes 2949120 | tf_op jit(solution)/shard_map/reduce_scatter | solution.py:389
  (144 other events, 2428.9 us)
Sparse Core Ops, SparseCore 0:
  10.4 30.4 all-gather.8
  43.1 67.6 all-gather.6
  112.4 89.3 all-gather.10
  203.3 29.3 all-gather.12
  234.1 46.8 all-gather.14
  497.7 33.1 reduce-scatter.20
  533.2 47.8 reduce-scatter.22
  583.4 87.7 reduce-scatter.26
  673.5 120.1 reduce-scatter.30
  795.9 186.2 reduce-scatter.16
  988.8 131.0 all-reduce.5
  1123.4 23.5 reduce-scatter.32
  1150.1 24.7 reduce-scatter.24
  1177.6 27.6 reduce-scatter.28
  1208.4 30.9 reduce-scatter.14
  1242.6 37.3 reduce-scatter.18
where the time goes:
time: 1300 us; the launch traced here: 1290 us
  waiting for transfers between devices  704 us (54%)
  matrix products  216 us (17%)
  local copies, waits for them, and re-layouts  150 us (12%)
  blocking collectives  101 us (8%)
  other arithmetic  99.2 us (8%)
  between operations  18.4 us (1%)
    reduce_scatter x1, waiting for transfers between devices, body(): lax.psum_scatter(grad_enc_ffn, 'col', scatter_dimension=2, tiled=True)  185 us
    unnamed x18, waiting for transfers between devices  145 us
    psum x1, waiting for transfers between devices, body(): lax.psum((grad_head, grad_smalls, loss_local), ('row', 'col'))  98.6 us
    dot_general x11, matrix products, product_of(): return jnp.dot(left, right, preferred_element_type=high_type)  81.4 us
    all_gather x1, waiting for transfers between devices, body(): lax.all_gather(rowed[1], 'col', axis=2, tiled=True)  71.9 us
    reduce_scatter x1, waiting for transfers between devices, body(): lax.psum_scatter(grad_dec_ffn, 'col', scatter_dimension=2, tiled=True)  43.8 us
    psum x1, blocking collectives, body(): lax.psum((grad_head, grad_smalls, loss_local), ('row', 'col'))  38.4 us
    reduce_scatter x1, waiting for transfers between devices, body(): lax.psum_scatter(col_enc_ffn, 'row', scatter_dimension=1, tiled=True)  38.4 us
  transfers between devices with their start and end apart: 16, of which 13 were waited for; matrix products, arithmetic and copies ran while one was open for 20% of the time, Pallas kernels for 0%

commit v1 on v0

--- a/solution.py
+++ b/solution.py
@@ -1,8 +1,11 @@
+import functools
 import math
 
 import jax
 import jax.numpy as jnp
 from jax import lax
+from jax.experimental import pallas as pl
+from jax.experimental.pallas import tpu as pltpu
 from jax.sharding import PartitionSpec as P
 
 D = 768
@@ -21,6 +24,625 @@
 norm_eps = 1e-06
 low_type = jnp.bfloat16
 high_type = jnp.float32
+
+
+MESH = pl.DeviceIdType.MESH
+
+
+def gather_kernel(depth, rows, half, own, out, zs, zr, xs, xr, ys, yr, dxs, dxr, dys, dyr, cs, cr, local):
+    row = lax.axis_index("row")
+    col = lax.axis_index("col")
+    y, x, z, k = row // 2, row % 2, col // 2, col % 2
+    row_x = y * 2 + (1 - x)
+    row_y = (1 - y) * 2 + x
+    row_d = (1 - y) * 2 + (1 - x)
+    near_x, near_y = (row_x, col), (row_y, col)
+    twin = (row, z * 2 + (1 - k))
+    lower, upper = (row, col - 2), (row, col + 2)
+    has_lower, has_upper = z > 0, z < depth - 1
+
+    barrier = pltpu.get_barrier_semaphore()
+    for other in (near_x, near_y, twin):
+        pl.semaphore_signal(barrier, inc=1, device_id=other, device_id_type=MESH)
+
+    @pl.when(has_lower)
+    def _():
+        pl.semaphore_signal(barrier, inc=1, device_id=lower, device_id_type=MESH)
+
+    @pl.when(has_upper)
+    def _():
+        pl.semaphore_signal(barrier, inc=1, device_id=upper, device_id_type=MESH)
+
+    pl.semaphore_wait(barrier, 3 + jnp.where(has_lower, 1, 0) + jnp.where(has_upper, 1, 0))
+
+    levels = [(0, 0)] + [(d, way) for d in range(1, depth) for way in (0, 1)]
+    level_of = {item: number for number, item in enumerate(levels)}
+    first, second = pl.ds(0, half), pl.ds(half, rows - half)
+
+    def place(level):
+        d, way = level
+        return z - d if way == 0 else z + d
+
+    def valid(level):
+        d, way = level
+        return z - d >= 0 if way == 0 else z + d < depth
+
+    def slot(level, row_now):
+        return out.at[place(level) * 2 + k, row_now]
+
+    def source(level):
+        return own if level == (0, 0) else slot(level, row)
+
+    def copy(src, dst, send, recv, target):
+        return pltpu.make_async_remote_copy(
+            src_ref=src, dst_ref=dst, send_sem=send, recv_sem=recv, device_id=target, device_id_type=MESH
+        )
+
+    def z_copy(level, way):
+        d = level[0]
+        src = source(level)
+        dst = out.at[place(level) * 2 + k, row]
+        n = level_of[level]
+        return copy(src, dst, zs.at[n, way], zr.at[d, way], upper if way == 0 else lower)
+
+    def x_copy(level):
+        n = level_of[level]
+        return copy(source(level), slot(level, row), xs.at[n], xr.at[n], near_x)
+
+    def y_copy(level):
+        n = level_of[level]
+        return copy(source(level), slot(level, row), ys.at[n], yr.at[n], near_y)
+
+    def dx_copy(level):
+        n = level_of[level]
+        ref = slot(level, row_y).at[second]
+        return copy(ref, ref, dxs.at[n], dxr.at[n], near_x)
+
+    def dy_copy(level):
+        n = level_of[level]
+        ref = slot(level, row_x).at[first]
+        return copy(ref, ref, dys.at[n], dyr.at[n], near_y)
+
+    def twin_copy(level, kind):
+        n = level_of[level]
+        src = (source(level), slot(level, row_x), slot(level, row_y), slot(level, row_d))[kind]
+        dst = slot(level, (row, row_x, row_y, row_d)[kind])
+        return copy(src, dst, cs.at[n, kind], cr.at[n, kind], twin)
+
+    def guarded(level, action):
+        if level == (0, 0):
+            action()
+        else:
+            pl.when(valid(level))(action)
+
+    def spread(level):
+        d, way = level
+
+        def action():
+            if level != (0, 0):
+                z_copy((d - 1, way if d > 1 else 0), way).wait_recv()
+            for direction in (0, 1):
+                if level == (0, 0) or direction == way:
+                    @pl.when(has_upper if direction == 0 else has_lower)
+                    def _():
+                        z_copy(level, direction).start()
+            x_copy(level).start()
+            y_copy(level).start()
+            twin_copy(level, 0).start()
+
+        guarded(level, action)
+
+    def turn(level):
+        def action():
+            x_copy(level).wait_recv()
+            dy_copy(level).start()
+            twin_copy(level, 1).start()
+            y_copy(level).wait_recv()
+            dx_copy(level).start()
+            twin_copy(level, 2).start()
+
+        guarded(level, action)
+
+    def close(level):
+        def action():
+            dx_copy(level).wait_recv()
+            dy_copy(level).wait_recv()
+            twin_copy(level, 3).start()
+
+        guarded(level, action)
+
+    def drain(level):
+        d, way = level
+
+        def action():
+            for direction in (0, 1):
+                if level == (0, 0) or direction == way:
+                    @pl.when(has_upper if direction == 0 else has_lower)
+                    def _():
+                        z_copy(level, direction).wait_send()
+            x_copy(level).wait_send()
+            y_copy(level).wait_send()
+            dx_copy(level).wait_send()
+            dy_copy(level).wait_send()
+            for kind in range(4):
+                twin_copy(level, kind).wait()
+
+        guarded(level, action)
+
+    keep = pltpu.make_async_copy(own, out.at[col, row], local)
+    keep.start()
+    for step in range(depth + 2):
+        for level in levels:
+            if level[0] == step:
+                spread(level)
+        for level in levels:
+            if level[0] == step - 1:
+                turn(level)
+        for level in levels:
+            if level[0] == step - 2:
+                close(level)
+    keep.wait()
+    for level in levels:
+        drain(level)
+
+
+def gather_blocks(own, depth):
+    rows, lanes = own.shape
+    half = (rows // 32) * 16
+    count = 2 * depth - 1
+    dma = pltpu.SemaphoreType.DMA
+    anywhere = pl.BlockSpec(memory_space=pltpu.HBM)
+    return pl.pallas_call(
+        functools.partial(gather_kernel, depth, rows, half),
+        out_shape=jax.ShapeDtypeStruct((2 * depth, 4, rows, lanes), own.dtype),
+        in_specs=[anywhere],
+        out_specs=anywhere,
+        scratch_shapes=[dma((count, 2)), dma((depth, 2))]
+        + [dma((count,)) for _ in range(8)]
+        + [dma((count, 4)), dma((count, 4)), dma],
+        compiler_params=pltpu.CompilerParams(collective_id=0, has_side_effects=True),
+        name="gather_blocks",
+    )(own)
+
+
+def far_first(depth):
+    orders = []
+    for z in range(depth):
+        orders.append(sorted(range(depth), key=lambda t: (-abs(t - z), -abs(2 * t - depth + 1))))
+    return orders
+
+
+code_type = jnp.int16
+code_top = 32767.0
+
+
+def encode(values):
+    peak = jnp.max(jnp.abs(values), axis=0, keepdims=True)
+    unit = jnp.maximum(peak, 1e-30) * (1.0 / code_top)
+    codes = jnp.round(values * (1.0 / unit))
+    codes = jnp.clip(codes, -code_top, code_top)
+    return codes.astype(jnp.int32).astype(code_type), unit
+
+
+def decode(codes, unit):
+    return codes.astype(jnp.int32).astype(high_type) * unit
+
+
+def reduce_kernel(depth, devices, cols, parts, chunk, half, blob, small, out, small_out,
+                  arrived, mine, stage_x, stage_y, recv_x, recv_y, turn_x, turn_y, back_x, back_y, line_out, line,
+                  units_out, units_in, line_units, box,
+                  s_load, s_cs, s_cr, s_xs, s_xr, s_ys, s_yr, s_txs, s_txr, s_tys, s_tyr, s_zs, s_zr,
+                  u_xs, u_xr, u_ys, u_yr, u_txs, u_txr, u_tys, u_tyr, u_zs, u_zr,
+                  s_ps, s_pr, s_qs, s_qr):
+    row = lax.axis_index("row")
+    col = lax.axis_index("col")
+    y, x, z, k = row // 2, row % 2, col // 2, col % 2
+    me = row * cols + col
+    near_x, near_y = (y * 2 + (1 - x), col), ((1 - y) * 2 + x, col)
+    twin = (row, z * 2 + (1 - k))
+    lower, upper = (row, col - 2), (row, col + 2)
+    has_lower, has_upper = z > 0, z < depth - 1
+    steps = depth * parts
+    slots = mine.shape[0]
+    ahead = slots - 1
+    a_rows, b_rows = pl.ds(0, half), pl.ds(half, chunk - half)
+
+    def device(offset):
+        index = (me + offset) % devices
+        return (index // cols, index % cols)
+
+    barrier = pltpu.get_barrier_semaphore()
+    for offset in range(1, devices):
+        pl.semaphore_signal(barrier, inc=1, device_id=device(offset), device_id_type=MESH)
+    pl.semaphore_wait(barrier, devices - 1)
+
+    def copy(src, dst, send, recv, target):
+        return pltpu.make_async_remote_copy(
+            src_ref=src, dst_ref=dst, send_sem=send, recv_sem=recv, device_id=target, device_id_type=MESH
+        )
+
+    class Pair:
+        def __init__(self, *copies):
+            self.copies = copies
+
+        def start(self):
+            for item in self.copies:
+                item.start()
+
+        def wait_recv(self):
+            for item in self.copies:
+                item.wait_recv()
+
+        def wait_send(self):
+            for item in self.copies:
+                item.wait_send()
+
+    orders = far_first(depth)
+
+    def goal(t):
+        turn = t // parts
+        value = 0
+        for a in range(depth):
+            for b in range(depth):
+                value = jnp.where((z == a) & (turn == b), orders[a][b], value)
+        return value
+
+    def span(t):
+        return pl.ds(pl.multiple_of((t % parts) * chunk, 16), chunk)
+
+    def load(t):
+        return pltpu.make_async_copy(
+            blob.at[goal(t) * 2 + k, :, span(t)], mine.at[t % slots], s_load.at[t % slots]
+        )
+
+    def core(t):
+        return copy(blob.at[goal(t) * 2 + (1 - k), :, span(t)], arrived.at[t], s_cs.at[t], s_cr.at[t], twin)
+
+    def paired(kind, src, dst, send, recv, unit_send, unit_recv, target):
+        def make(t):
+            return Pair(
+                copy(src.at[t], dst.at[t], send.at[t], recv.at[t], target),
+                copy(units_out.at[t, kind], units_in.at[t, kind], unit_send.at[t], unit_recv.at[t], target),
+            )
+
+        return make
+
+    first_x = paired(0, stage_x, recv_x, s_xs, s_xr, u_xs, u_xr, near_x)
+    first_y = paired(1, stage_y, recv_y, s_ys, s_yr, u_ys, u_yr, near_y)
+    second_x = paired(2, turn_x, back_x, s_txs, s_txr, u_txs, u_txr, near_x)
+    second_y = paired(3, turn_y, back_y, s_tys, s_tyr, u_tys, u_tyr, near_y)
+
+    def along(t, index, target):
+        return Pair(
+            copy(line_out.at[t], line.at[index], s_zs.at[t], s_zr.at[index], target),
+            copy(units_out.at[t, 4], line_units.at[index], u_zs.at[t], u_zr.at[index], target),
+        )
+
+    def upper_index(t):
+        return (goal(t) + 1) * parts + t % parts
+
+    def lower_index(t):
+        return goal(t) * parts + t % parts
+
+    def to_upper(t):
+        return along(t, upper_index(t), upper)
+
+    def to_lower(t):
+        return along(t, lower_index(t), lower)
+
+    def small_send(offset):
+        target = device(offset)
+        return copy(small.at[target[0] * cols + target[1]], box.at[offset], s_ps.at[offset], s_pr.at[offset], target)
+
+    def small_back(offset):
+        return copy(small_out.at[me], small_out.at[me], s_qs.at[offset], s_qr.at[offset], device(offset))
+
+    def small_back_recv(offset):
+        origin = (me + devices - offset) % devices
+        return copy(small_out.at[origin], small_out.at[origin], s_qs.at[offset], s_qr.at[offset], device(offset))
+
+    for t in range(ahead):
+        load(t).start()
+        core(t).start()
+    for offset in range(1, devices):
+        small_send(offset).start()
+
+    def stage_one(t):
+        load(t).wait()
+        core(t).wait_recv()
+        slot = t % slots
+        for other in (0, 1):
+            away = other * 2 + (1 - x)
+            stay = other * 2 + x
+            codes, unit = encode(mine[slot, away, a_rows] + arrived[t, away, a_rows])
+            stage_x[t, other] = codes
+            units_out[t, 0, pl.ds(other, 1)] = unit
+            arrived[t, stay, a_rows] += mine[slot, stay, a_rows]
+        first_x(t).start()
+        for other in (0, 1):
+            away = (1 - y) * 2 + other
+            stay = y * 2 + other
+            codes, unit = encode(mine[slot, away, b_rows] + arrived[t, away, b_rows])
+            stage_y[t, other] = codes
+            units_out[t, 1, pl.ds(other, 1)] = unit
+            arrived[t, stay, b_rows] += mine[slot, stay, b_rows]
+        first_y(t).start()
+
+    def stage_two(t):
+        first_x(t).wait_recv()
+        away = (1 - y) * 2 + x
+        codes, unit = encode(arrived[t, away, a_rows] + decode(recv_x[t, 1 - y], units_in[t, 0, pl.ds(1 - y, 1)]))
+        turn_y[t] = codes
+        units_out[t, 3, pl.ds(0, 1)] = unit
+        second_y(t).start()
+        arrived[t, row, a_rows] += decode(recv_x[t, y], units_in[t, 0, pl.ds(y, 1)])
+        first_y(t).wait_recv()
+        away = y * 2 + (1 - x)
+        codes, unit = encode(arrived[t, away, b_rows] + decode(recv_y[t, 1 - x], units_in[t, 1, pl.ds(1 - x, 1)]))
+        turn_x[t] = codes
+        units_out[t, 2, pl.ds(0, 1)] = unit
+        second_x(t).start()
+        arrived[t, row, b_rows] += decode(recv_y[t, x], units_in[t, 1, pl.ds(x, 1)])
+
+    def stage_three(t):
+        second_y(t).wait_recv()
+        arrived[t, row, a_rows] += decode(back_y[t], units_in[t, 3, pl.ds(0, 1)])
+        second_x(t).wait_recv()
+        arrived[t, row, b_rows] += decode(back_x[t], units_in[t, 2, pl.ds(0, 1)])
+
+    def take(index):
+        return decode(line[index], line_units[index, pl.ds(0, 1)])
+
+    def pack(t):
+        codes, unit = encode(arrived[t, row])
+        line_out[t] = codes
+        units_out[t, 4, pl.ds(0, 1)] = unit
+
+    def stage_four(t):
+        target = goal(t)
+
+        @pl.when((target >= z) & has_lower)
+        def _():
+            to_upper(t).wait_recv()
+            arrived[t, row] += take(upper_index(t))
+
+        @pl.when((target <= z) & has_upper)
+        def _():
+            to_lower(t).wait_recv()
+            arrived[t, row] += take(lower_index(t))
+
+        @pl.when(target != z)
+        def _():
+            pack(t)
+
+        @pl.when(target > z)
+        def _():
+            to_upper(t).start()
+
+        @pl.when(target < z)
+        def _():
+            to_lower(t).start()
+
+        @pl.when(target == z)
+        def _():
+            out[span(t)] = arrived[t, row]
+
+    lags = (2, 4, 6)
+
+    def body(i, carry):
+        @pl.when(i + ahead < steps)
+        def _():
+            load(i + ahead).start()
+            core(i + ahead).start()
+
+        @pl.when(i < steps)
+        def _():
+            stage_one(i)
+
+        for lag, stage in zip(lags, (stage_two, stage_three, stage_four)):
+            @pl.when((i >= lag) & (i - lag < steps))
+            def _():
+                stage(i - lag)
+
+        @pl.when(i == steps // 2)
+        def _():
+            total = small[me]
+            for offset in range(1, devices):
+                small_send(offset).wait_recv()
+                total = total + box[offset]
+            small_out[me] = total
+            for offset in range(1, devices):
+                small_back(offset).start()
+
+        return carry
+
+    lax.fori_loop(0, steps + lags[-1], body, 0)
+
+    def finish(t, carry):
+        core(t).wait_send()
+        first_x(t).wait_send()
+        first_y(t).wait_send()
+        second_x(t).wait_send()
+        second_y(t).wait_send()
+
+        @pl.when(goal(t) > z)
+        def _():
+            to_upper(t).wait_send()
+
+        @pl.when(goal(t) < z)
+        def _():
+            to_lower(t).wait_send()
+
+        return carry
+
+    lax.fori_loop(0, steps, finish, 0)
+    for offset in range(1, devices):
+        small_send(offset).wait_send()
+        small_back(offset).wait_send()
+        small_back_recv(offset).wait_recv()
+
+
+def reduce_blocks(blob, small, depth, parts):
+    cols, _, rows, lanes = blob.shape
+    devices = 4 * cols
+    chunk = rows // parts
+    half = -(-chunk // 32) * 16
+    rest = chunk - half
+    steps = depth * parts
+    lines = (depth + 1) * parts
+    dma = pltpu.SemaphoreType.DMA
+    vm = pltpu.VMEM
+    return pl.pallas_call(
+        functools.partial(reduce_kernel, depth, devices, cols, parts, chunk, half),
+        out_shape=(
+            jax.ShapeDtypeStruct((rows, lanes), high_type),
+            jax.ShapeDtypeStruct(small.shape, high_type),
+        ),
+        in_specs=[pl.BlockSpec(memory_space=pltpu.HBM), pl.BlockSpec(memory_space=pltpu.VMEM)],
+        out_specs=[pl.BlockSpec(memory_space=pltpu.VMEM)] * 2,
+        scratch_shapes=[
+            vm((steps, 4, chunk, lanes), high_type),
+            vm((4, 4, chunk, lanes), high_type),
+            vm((steps, 2, half, lanes), code_type),
+            vm((steps, 2, rest, lanes), code_type),
+            vm((steps, 2, half, lanes), code_type),
+            vm((steps, 2, rest, lanes), code_type),
+            vm((steps, rest, lanes), code_type),
+            vm((steps, half, lanes), code_type),
+            vm((steps, rest, lanes), code_type),
+            vm((steps, half, lanes), code_type),
+            vm((steps, chunk, lanes), code_type),
+            vm((lines, chunk, lanes), code_type),
+            vm((steps, 5, 8, lanes), high_type),
+            vm((steps, 4, 8, lanes), high_type),
+            vm((lines, 8, lanes), high_type),
+            vm((devices,) + small.shape[1:], high_type),
+            dma((4,)),
+        ]
+        + ([dma((steps,)) for _ in range(11)] + [dma((lines,))])
+        + ([dma((steps,)) for _ in range(9)] + [dma((lines,))])
+        + [dma((devices,)) for _ in range(4)],
+        compiler_params=pltpu.CompilerParams(
+            collective_id=1, has_side_effects=True, vmem_limit_bytes=62 << 20
+        ),
+        name="reduce_blocks",
+    )(blob, small)
+
+
+LANES = 128
+
+
+def tiles_of(block):
+    rows, width = block.shape
+    tiles = -(-width // LANES)
+    block = jnp.pad(block, ((0, 0), (0, tiles * LANES - width)))
+    return block.reshape(rows, tiles, LANES).transpose(1, 0, 2).reshape(tiles * rows, LANES)
+
+
+def untile(block, rows, width):
+    tiles = -(-width // LANES)
+    return block.reshape(tiles, rows, LANES).transpose(1, 0, 2).reshape(rows, tiles * LANES)[:, :width]
+
+
+def fold_proj(block):
+    half = block.shape[0] // 2
+    return jnp.concatenate([block[:half], block[half:]], 1)
+
+
+def unfold_proj(block):
+    width = block.shape[1] // 2
+    return jnp.concatenate([block[:, :width], block[:, width:]], 0)
+
+
+def pack_shards(enc_w, enc_ffn, dec_proj, dec_w, dec_ffn):
+    return jnp.concatenate(
+        [
+            tiles_of(enc_w),
+            tiles_of(enc_ffn[0]),
+            tiles_of(enc_ffn[1]),
+            tiles_of(dec_w),
+            tiles_of(dec_ffn[0]),
+            tiles_of(dec_ffn[1]),
+            fold_proj(dec_proj),
+        ],
+        0,
+    )
+
+
+def unpack_shards(blob):
+    cuts = [0, 768, 576, 576, 256, 256, 256, 96]
+    places = [sum(cuts[: index + 1]) for index in range(len(cuts))]
+    piece = [blob[places[index] : places[index + 1]] for index in range(7)]
+    return (
+        untile(piece[0], 192, 480),
+        jnp.stack([untile(piece[1], 192, 384), untile(piece[2], 192, 384)]),
+        unfold_proj(piece[6]),
+        untile(piece[3], 128, 256),
+        jnp.stack([untile(piece[4], 128, 256), untile(piece[5], 128, 256)]),
+    )
+
+
+def whole_blob(enc, enc_ffn, proj, dec, dec_ffn, row_size, col_size):
+    def blocks(array):
+        rows, width = array.shape[0] // row_size, array.shape[1] // col_size
+        return array.reshape(row_size, rows, col_size, width).transpose(2, 0, 1, 3)
+
+    def tiled(array):
+        cut = blocks(array)
+        return jax.vmap(jax.vmap(tiles_of))(cut)
+
+    return jnp.concatenate(
+        [
+            tiled(enc),
+            tiled(enc_ffn[0]),
+            tiled(enc_ffn[1]),
+            tiled(dec),
+            tiled(dec_ffn[0]),
+            tiled(dec_ffn[1]),
+            jax.vmap(jax.vmap(fold_proj))(blocks(proj)),
+        ],
+        2,
+    )
+
+
+def whole_arrays(blob):
+    col_size, row_size = blob.shape[:2]
+    parts = jax.vmap(jax.vmap(unpack_shards))(blob)
+
+    def joined(array):
+        if array.ndim == 4:
+            return array.transpose(1, 2, 0, 3).reshape(row_size * array.shape[2], col_size * array.shape[3])
+        return array.transpose(2, 1, 3, 0, 4).reshape(2, row_size * array.shape[3], col_size * array.shape[4])
+
+    return tuple(joined(item) for item in parts)
+
+
+def gather_weights(enc_w, enc_ffn, dec_proj, dec_w, dec_ffn):
+    shards = (enc_w, enc_ffn, dec_proj, dec_w, dec_ffn)
+    if lax.axis_size("row") == 4 and lax.axis_size("col") == 8:
+        own = pack_shards(*[item.astype(low_type) for item in shards])
+        return whole_arrays(gather_blocks(own, lax.axis_size("col") // 2))
+    full = []
+    for item in shards:
+        rowed = lax.all_gather(item.astype(low_type), "row", axis=item.ndim - 2, tiled=True)
+        full.append(lax.all_gather(rowed, "col", axis=item.ndim - 1, tiled=True))
+    return tuple(full)
+
+
+def reduce_grads(grads, smalls, loss):
+    count = smalls.shape[0]
+    if lax.axis_size("row") == 4 and lax.axis_size("col") == 8:
+        blob = whole_blob(*grads, 4, 8)
+        small = jnp.concatenate([smalls, loss[None], jnp.zeros((32 * 8 * LANES - count - 1,), high_type)])
+        summed, small = reduce_blocks(blob, small.reshape(32, 8, LANES), 4, 6)
+        small = small.reshape(-1)
+        return unpack_shards(summed), small[:count], small[count]
+    shards = []
+    for item in grads:
+        done = lax.psum_scatter(item, "col", scatter_dimension=item.ndim - 1, tiled=True)
+        shards.append(lax.psum_scatter(done, "row", scatter_dimension=item.ndim - 2, tiled=True))
+    smalls, loss = lax.psum((smalls, loss), ("row", "col"))
+    return tuple(shards), smalls, loss
 
 
 def product_of(left, right):
@@ -256,19 +878,8 @@
     second_head_w,
     second_smalls,
 ):
-    rowed = (
-        lax.all_gather(enc_w.astype(low_type), "row", axis=0, tiled=True),
-        lax.all_gather(enc_ffn.astype(low_type), "row", axis=1, tiled=True),
-        lax.all_gather(dec_proj.astype(low_type), "row", axis=0, tiled=True),
-        lax.all_gather(dec_w.astype(low_type), "row", axis=0, tiled=True),
-        lax.all_gather(dec_ffn.astype(low_type), "row", axis=1, tiled=True),
-    )
-    enc_full, enc_ffn_w, proj_full, dec_full, dec_ffn_w = (
-        lax.all_gather(rowed[0], "col", axis=1, tiled=True),
-        lax.all_gather(rowed[1], "col", axis=2, tiled=True),
-        lax.all_gather(rowed[2], "col", axis=1, tiled=True),
-        lax.all_gather(rowed[3], "col", axis=1, tiled=True),
-        lax.all_gather(rowed[4], "col", axis=2, tiled=True),
+    enc_full, enc_ffn_w, proj_full, dec_full, dec_ffn_w = gather_weights(
+        enc_w, enc_ffn, dec_proj, dec_w, dec_ffn
     )
     head_low = head_w.astype(low_type)
     enc_vec, enc_up, dec_vec, dec_up, head_bias = unpack(smalls)
@@ -313,7 +924,7 @@
     loss_local = jnp.sum(weight_mask * error * error)
     count = batch * lax.axis_size("row") * lax.axis_size("col") * (PATCHES - KEEP) * P_SIZE
     grad_predict = (2.0 * weight_mask * error / count).astype(low_type)
-    grad_head = weight_grad(final, grad_predict)
+    summed_head = lax.psum(weight_grad(final, grad_predict), ("row", "col"))
     grad_final = against_rows(grad_predict, head_low)
     grad_patch_rows, dec_gain, dec_shift = norm_back(
         patch_rows, dec_vec[10], dec_vec[11], grad_final
@@ -377,22 +988,8 @@
         ]
     )
     grad_enc_full = jnp.concatenate([grad_patch, grad_enc_wide], 1)
-    col_enc, col_enc_ffn, col_proj, col_dec, col_dec_ffn = (
-        lax.psum_scatter(grad_enc_full, "col", scatter_dimension=1, tiled=True),
-        lax.psum_scatter(grad_enc_ffn, "col", scatter_dimension=2, tiled=True),
-        lax.psum_scatter(grad_proj, "col", scatter_dimension=1, tiled=True),
-        lax.psum_scatter(grad_dec_wide, "col", scatter_dimension=1, tiled=True),
-        lax.psum_scatter(grad_dec_ffn, "col", scatter_dimension=2, tiled=True),
-    )
-    sharded = (
-        lax.psum_scatter(col_enc, "row", scatter_dimension=0, tiled=True),
-        lax.psum_scatter(col_enc_ffn, "row", scatter_dimension=1, tiled=True),
-        lax.psum_scatter(col_proj, "row", scatter_dimension=0, tiled=True),
-        lax.psum_scatter(col_dec, "row", scatter_dimension=0, tiled=True),
-        lax.psum_scatter(col_dec_ffn, "row", scatter_dimension=1, tiled=True),
-    )
-    summed_head, summed_smalls, loss_sum = lax.psum(
-        (grad_head, grad_smalls, loss_local), ("row", "col")
+    sharded, summed_smalls, loss_sum = reduce_grads(
+        (grad_enc_full, grad_enc_ffn, grad_proj, grad_dec_wide, grad_dec_ffn), grad_smalls, loss_local
     )
     grads = (sharded[0], sharded[1], sharded[2], sharded[3], sharded[4], summed_head, summed_smalls)
     params = (enc_w, enc_ffn, dec_proj, dec_w, dec_ffn, head_w, smalls)

time: 1300 us -> 1130 us (0.87)
  waiting for transfers between devices: 704 us -> 0.02 us
  local copies, waits for them, and re-layouts: 150 us -> 526 us
  Pallas kernels: 0 us -> 219 us
  blocking collectives: 101 us -> 0 us
  other arithmetic: 99.2 us -> 125 us
    reduce_scatter x8 -> x0, waiting for transfers between devices: 354 us -> none  [the longest x1 185 us: body(): lax.psum_scatter(grad_enc_ffn, 'col', scatter_dimension=2, tiled=True)]
    pallas_call x0 -> x2, Pallas kernels: none -> 219 us  [the longest x1 117 us: reduce_blocks(): pl.pallas_call(functools.partial(reduce_kernel, depth, devices, cols, par...]
    reshape x0 -> x29, local copies, waits for them, and re-layouts: none -> 182 us  [the longest x12 55.4 us: tiles_of(): block.reshape(rows, tiles, LANES).transpose(1, 0, 2)]
    unnamed x18 -> x1, waiting for transfers between devices: 145 us -> 0.02 us
    all_gather x5 -> x0, waiting for transfers between devices: 107 us -> none  [the longest x1 71.9 us: body(): lax.all_gather(rowed[1], 'col', axis=2, tiled=True)]
    psum x1, waiting for transfers between devices: 98.6 us -> 0.01 us  [body(): summed_head = lax.psum(weight_grad(final, grad_predict), ('row', 'col'))]
    all_gather x5 -> x0, blocking collectives: 62.9 us -> none  [the longest x1 20.9 us: body(): lax.all_gather(rowed[2], 'col', axis=1, tiled=True)]
    unnamed x313 -> x408, local copies, waits for them, and re-layouts: 35.7 us -> 95 us
  transfers between devices with their start and end apart: 16 -> 1, of which waited for: 13 -> 0; matrix products, arithmetic and copies ran while one was open for 20% -> 47% of each run, Pallas kernels for 0% -> 11%
where the time goes in v1:
time: 1130 us; the launch traced here: 1110 us
  local copies, waits for them, and re-layouts  526 us (47%)
  matrix products  226 us (20%)
  Pallas kernels  219 us (19%)
  other arithmetic  125 us (11%)
  between operations  19.3 us (2%)
    pallas_call x1, Pallas kernels, reduce_blocks(): pl.pallas_call(functools.partial(reduce_kernel, depth, devices, cols, par...  117 us
    pallas_call x1, Pallas kernels, gather_blocks(): pl.pallas_call(functools.partial(gather_kernel, depth, rows, half), out_s...  102 us
    unnamed x408, local copies, waits for them, and re-layouts  95 us
    dot_general x11, matrix products, product_of(): return jnp.dot(left, right, preferred_element_type=high_type)  75.9 us
    reshape x12, local copies, waits for them, and re-layouts, tiles_of(): block.reshape(rows, tiles, LANES).transpose(1, 0, 2)  55.4 us
    reshape x10, local copies, waits for them, and re-layouts, untile(): block.reshape(tiles, rows, LANES).transpose(1, 0, 2)  48.7 us
    dot_general x11, matrix products, weight_grad(): lax.dot_general(left, right, (((0,), (0,)), ((), ())), preferred_element_...  42.7 us
    transpose x7, local copies, waits for them, and re-layouts, tiles_of(): block.reshape(rows, tiles, LANES).transpose(1, 0, 2)  41.2 us
  transfers between devices with their start and end apart: 1, of which 0 were waited for; matrix products, arithmetic and copies ran while one was open for 47% of the time, Pallas kernels for 11%

profile of v1, /device:TPU:0, one launch (start us, length us, event | category | flops | bytes accessed | tf_op | source)
XLA Modules:
  0.0 1114.3 jit_solution(16034610510988435206)
XLA Ops:
  11.5 102.0 %gather_blocks.1 = bf16[8,4,2784,128]{3,2,1,0:T(8,128)(2,1)} custom-call(bf16[2784,128]{1,0:T(8,128)(2,1)} %copy-done.77), custom_call_target="tpu_custom_call" | custom-call | tf_op jit(solution)/shard_map/gather_blocks/pallas_call | solution.py:195
  124.9 10.3 reshape.953
  145.0 13.2 %reshape.954 = bf16[768,3840]{1,0:T(8,128)(2,1)} reshape(bf16[4,192,8,480]{3,2,1,0:T(8,128)(2,1)} %copy.190) | data formatting | bytes 11796480 | tf_op jit(solution)/shard_map/reshape | solution.py:614
  205.4 12.9 %reshape.961 = bf16[1,8,4,192,384]{4,3,2,1,0:T(8,128)(2,1)} reshape(bf16[8,4,192,3,128]{4,3,2,1,0:T(4,128)(2,1)} %bitcast.366) | data formatting | bytes 9437184 | tf_op jit(solution)/shard_map/vmap(vmap())/stack;vmap(vmap())/reshape | solution.py:578
  227.8 13.1 %reshape.963 = bf16[1,8,4,192,384]{4,3,2,1,0:T(8,128)(2,1)} reshape(bf16[8,4,192,3,128]{4,3,2,1,0:T(4,128)(2,1)} %bitcast.367) | data formatting | bytes 9437184 | tf_op jit(solution)/shard_map/vmap(vmap())/stack;vmap(vmap())/reshape | solution.py:578
  262.3 11.6 %multiply_convert_fusion.3 = (bf16[300,3072]{1,0:T(8,128)(2,1)S(1)}, f32[300,3072]{1,0:T(8,128)}, f32[300,3072]{1,0:T(8,128)}) fusion(f32[3072]{0:T(1024)S(1)} %slice-done.11, bf16[768,3072]{1,0:T(8,128)(2,1)S(1)} %bitcast.395, f32[300,768]{1,0:T(8,128)S(1)} %copy-done.23, f32[768]{0:T(1024)S(1)} %get-tuple-element.306, f32[768]{0:T(1024)S(1)} %get-tuple-element.307, ...), kind=kOutput, calls=%fused_computation.78 | convolution fusion | flops 1477555200 | bytes 14877024 | tf_op jit(solution)/shard_map/dot_general | solution.py:649
  323.1 11.0 fusion.189
  334.1 11.4 %fusion = f32[6,16,197]{2,1,0:T(8,128)S(1)} fusion(f32[6,16,197,197]{2,3,1,0:T(8,128)} %get-tuple-element.342, f32[6,16,197]{2,1,0:T(8,128)S(1)} %get-tuple-element.341), kind=kLoop, calls=%fused_computation.5 | loop fusion | flops 7432416 | bytes 15053952 | tf_op jit(solution)/shard_map/reduce_sum | solution.py:725
  389.7 24.3 %fusion.6 = (f32[1182,2048]{1,0:T(8,128)}, f32[1182,2048]{1,0:T(8,128)S(1)}) fusion(f32[2048]{0:T(1024)S(1)} %slice.500, bf16[512,2048]{1,0:T(8,128)(2,1)S(1)} %bitcast.406, f32[1182,512]{1,0:T(8,128)S(1)} %get-tuple-element.344, f32[512]{0:T(512)S(1)} %copy-done.132, f32[512]{0:T(512)S(1)} %copy-done.131, f32[1182]{0:T(1024)S(1)} %fusion.134, ...), kind=kOutput, calls=%fused_computation.14 | convolution fusion | flops 2634365952 | bytes 23905520 | tf_op jit(solution)/shard_map/dot_general | solution.py:649
  473.7 12.5 %convert_reduce_fusion = (f32[2048]{0:T(1024)}, bf16[1182,2048]{1,0:T(8,128)(2,1)S(1)}) fusion(f32[1182,2048]{1,0:T(8,128)} %get-tuple-element.345, bf16[1182,512]{1,0:T(8,128)(2,1)} %convert_element_type.286, bf16[512,2048]{1,0:T(8,128)(2,1)} %bitcast.384, f32[1182,2048]{1,0:T(8,128)} %copy-done.4, f32[2048]{0:T(1024)S(1)} %slice.500), kind=kOutput, calls=%fused_computation.23 | convolution fusion | flops 2519984128 | bytes 27531264 | tf_op jit(solution)/shard_map/dot_general | solution.py:649
  510.3 11.5 %fusion.68 = bf16[6,197,16,32]{1,3,2,0:T(8,128)(2,1)} fusion(f32[6,16,197,197]{2,3,1,0:T(8,128)} %get-tuple-element.342, f32[6,16,197]{2,1,0:T(8,128)S(1)} %log_add_fusion, bf16[6,197,16,32]{1,0,3,2:T(8,128)(2,1)} %reshape.982), kind=kOutput, calls=%fused_computation.161 | convolution fusion | flops 246499008 | bytes 17399040 | tf_op jit(solution)/shard_map/bhqk,bqhd->bkhd/dot_general | solution.py:794
  521.8 14.8 %multiply_reduce_fusion = (f32[6,16,197]{2,1,0:T(8,128)S(1)}, f32[6,16,197,197]{2,3,1,0:T(8,128)}) fusion(f32[6,16,197,197]{2,3,1,0:T(8,128)} %get-tuple-element.342, f32[6,16,197]{2,1,0:T(8,128)S(1)} %log_add_fusion, bf16[6,197,16,32]{1,0,3,2:T(8,128)(2,1)} %reshape.972, bf16[6,197,16,32]{1,0,3,2:T(8,128)(2,1)} %reshape.982), kind=kOutput, calls=%fused_computation.1 | convolution fusion | flops 249600576 | bytes 32377344 | tf_op jit(solution)/shard_map/bqhd,bkhd->bhqk/dot_general | solution.py:797
  536.6 13.8 %multiply_convert_fusion = bf16[6,16,197,197]{2,3,1,0:T(8,128)(2,1)S(1)} fusion(f32[6,16,197,197]{2,3,1,0:T(8,128)} %get-tuple-element.350, f32[6,16,197,197]{2,3,1,0:T(8,128)} %get-tuple-element.342, f32[6,16,197]{2,1,0:T(8,128)S(1)} %get-tuple-element.349, f32[6,16,197]{2,1,0:T(8,128)S(1)} %log_add_fusion), kind=kLoop, calls=%fused_computation | loop fusion | flops 14902656 | bytes 37407936 | tf_op jit(solution)/shard_map/convert_element_type | solution.py:802
  701.1 22.4 %fusion.9 = bf16[2048,1182]{0,1:T(8,128)(2,1)} fusion(f32[1182,2048]{1,0:T(8,128)S(1)} %bitcast.352, f32[2048]{0:T(1024)S(1)} %slice.500), kind=kLoop, calls=%fused_computation.17 | loop fusion | flops 159768576 | bytes 14532608 | tf_op jit(solution)/shard_map/convert_element_type | solution.py:741
  768.8 14.8 %reshape.995 = f32[8,4,192,3,128]{4,3,2,1,0:T(4,128)} reshape(f32[8,4,192,384]{3,2,1,0:T(8,128)} %bitcast.361) | data formatting | bytes 18874368 | tf_op jit(solution)/shard_map/vmap(vmap())/reshape | solution.py:539
  783.6 9.7 copy.241
  797.9 15.7 %reshape.992 = f32[4,192,8,480]{3,2,1,0:T(8,128)} reshape(f32[768,3840]{1,0:T(8,128)} %pad_maximum_fusion) | data formatting | bytes 23592960 | tf_op jit(solution)/shard_map/reshape | solution.py:588
  813.6 16.5 %copy.372 = f32[4,192,8,480]{3,1,0,2:T(8,128)} copy(f32[4,192,8,480]{3,2,1,0:T(8,128)} %reshape.992) | data formatting | bytes 23592960 | tf_op jit(solution)/shard_map/reshape | solution.py:588
  830.1 11.6 %pad.28 = f32[8,4,192,512]{3,2,1,0:T(8,128)} pad(f32[8,4,192,480]{3,2,1,0:T(8,128)} %bitcast.348, f32[]{:T(128)} %constant.392.clone.1), padding=0_0x0_0x0_0x0_32 | pad | bytes 24379396 | tf_op jit(solution)/shard_map/vmap(vmap(jit(_pad)))/pad | solution.py:538
  841.7 14.8 %reshape.993 = f32[8,4,192,4,128]{4,3,2,1,0:T(4,128)} reshape(f32[8,4,192,512]{3,2,1,0:T(8,128)} %pad.28) | data formatting | bytes 25165824 | tf_op jit(solution)/shard_map/vmap(vmap())/reshape | solution.py:539
  856.5 11.0 copy.239
  867.5 10.5 constant_dynamic-update-slice_fusion.18
  889.1 14.7 %reshape.997 = f32[8,4,192,3,128]{4,3,2,1,0:T(4,128)} reshape(f32[8,4,192,384]{3,2,1,0:T(8,128)} %bitcast.362) | data formatting | bytes 18874368 | tf_op jit(solution)/shard_map/vmap(vmap())/reshape | solution.py:539
  961.7 117.0 %reduce_blocks.1 = (f32[2784,128]{1,0:T(8,128)}, f32[32,8,128]{2,1,0:T(8,128)}) custom-call(f32[8,4,2784,128]{3,2,1,0:T(8,128)} %maximum_dynamic-update-slice_fusion.blob, f32[32,8,128]{2,1,0:T(8,128)} %bitcast.421), custom_call_target="tpu_custom_call" | custom-call | tf_op jit(solution)/shard_map/reduce_blocks/pallas_call | solution.py:495
  (711 shorter events, 574.0 us)
Async XLA Ops:
  7.2 1093.9 %all-reduce.7.cloned.1.call-start = ((), (), s32[]{:S(2)}) async-start(), calls=%async_computation | async-start | bytes 3145728 | tf_op jit(solution)/shard_map/psum | solution.py:927
  7.3 154.3 %copy-start.145 = (f32[196]{0:T(256)}, f32[196]{0:T(256)S(1)}, u32[]{:S(2)}) copy-start(f32[196]{0:T(256)S(1)} %get-tuple-element.359) | copy-start | bytes 2356
  7.3 154.3 %copy-start.147 = (f32[196]{0:T(256)}, f32[196]{0:T(256)S(1)}, u32[]{:S(2)}) copy-start(f32[196]{0:T(256)S(1)} %get-tuple-element.360) | copy-start | bytes 2356
  158.9 18.7 %copy-start.96 = (f32[768]{0:T(1024)}, f32[768]{0:T(1024)S(1)}, u32[]{:S(2)}) copy-start(f32[768]{0:T(1024)S(1)} %get-tuple-element.312) | copy-start | bytes 9220
  158.9 18.7 %copy-start.107 = (f32[768]{0:T(1024)}, f32[768]{0:T(1024)S(1)}, u32[]{:S(2)}) copy-start(f32[768]{0:T(1024)S(1)} %get-tuple-element.311) | copy-start | bytes 9220
  158.9 103.3 %copy-start.98 = (f32[768]{0:T(1024)}, f32[768]{0:T(1024)S(1)}, u32[]{:S(2)}) copy-start(f32[768]{0:T(1024)S(1)} %get-tuple-element.307) | copy-start | bytes 9220
  158.9 103.3 %copy-start.109 = (f32[768]{0:T(1024)}, f32[768]{0:T(1024)S(1)}, u32[]{:S(2)}) copy-start(f32[768]{0:T(1024)S(1)} %get-tuple-element.306) | copy-start | bytes 9220
  158.9 17.7 %copy-start.100 = (s32[6,49]{1,0:T(8,128)}, s32[6,49]{1,0:T(8,128)S(1)}, u32[]{:S(2)}) copy-start(s32[6,49]{1,0:T(8,128)S(1)} %slice.446) | copy-start | bytes 3532
  177.5 15.2 %copy-start.17 = (f32[300,768]{1,0:T(8,128)}, f32[300,768]{1,0:T(8,128)S(1)}, u32[]{:S(2)}) copy-start(f32[300,768]{1,0:T(8,128)S(1)} %reshape.956) | copy-start | bytes 2764804
  194.8 67.4 %copy-start.118 = (f32[300]{0:T(512)}, f32[300]{0:T(512)S(1)}, u32[]{:S(2)}) copy-start(f32[300]{0:T(512)S(1)} %broadcast_multiply_fusion.7) | copy-start | bytes 3604
  196.0 66.3 %copy-start.125 = (f32[300]{0:T(512)}, f32[300]{0:T(512)S(1)}, u32[]{:S(2)}) copy-start(f32[300]{0:T(512)S(1)} %fusion.137) | copy-start | bytes 3604
  288.0 15.8 %copy-start.127 = (f32[1182]{0:T(1024)}, f32[1182]{0:T(1024)S(1)}, u32[]{:S(2)}) copy-start(f32[1182]{0:T(1024)S(1)} %div.285) | copy-start | bytes 14188
  389.7 24.4 %copy-start.36 = (bf16[64,8,8,256]{3,1,2,0:T(8,128)(2,1)}, bf16[64,8,8,256]{3,1,2,0:T(8,128)(2,1)S(1)}, u32[]{:S(2)}) copy-start(bf16[64,8,8,256]{3,1,2,0:T(8,128)(2,1)S(1)} %copy.295) | copy-start | bytes 6291460
  389.7 27.9 %copy-start.149 = (f32[512]{0:T(512)S(1)}, f32[512]{0:T(512)}, u32[]{:S(2)}) copy-start(f32[512]{0:T(512)} %get-tuple-element.293) | copy-start | bytes 6148
  701.0 22.6 %copy-start.174 = (f32[512]{0:T(512)S(1)}, f32[512]{0:T(512)}, u32[]{:S(2)}) copy-start(f32[512]{0:T(512)} %get-tuple-element.192) | copy-start | bytes 6148
  701.0 22.6 %copy-start.173 = (f32[512]{0:T(512)S(1)}, f32[512]{0:T(512)}, u32[]{:S(2)}) copy-start(f32[512]{0:T(512)} %get-tuple-element.196) | copy-start | bytes 6148
  701.0 22.7 %copy-start.167 = (f32[512]{0:T(512)S(1)}, f32[512]{0:T(512)}, u32[]{:S(2)}) copy-start(f32[512]{0:T(512)} %get-tuple-element.188) | copy-start | bytes 6148
  701.0 22.7 %copy-start.168 = (f32[512]{0:T(512)S(1)}, f32[512]{0:T(512)}, u32[]{:S(2)}) copy-start(f32[512]{0:T(512)} %get-tuple-element.194) | copy-start | bytes 6148
  701.0 22.7 %copy-start.170 = (f32[512]{0:T(512)S(1)}, f32[512]{0:T(512)}, u32[]{:S(2)}) copy-start(f32[512]{0:T(512)} %get-tuple-element.190) | copy-start | bytes 6148
  701.0 22.7 %copy-start.171 = (f32[512]{0:T(512)S(1)}, f32[512]{0:T(512)}, u32[]{:S(2)}) copy-start(f32[512]{0:T(512)} %get-tuple-element.195) | copy-start | bytes 6148
  701.0 22.8 %copy-start.160 = (f32[768]{0:T(1024)S(1)}, f32[768]{0:T(1024)}, u32[]{:S(2)}) copy-start(f32[768]{0:T(1024)} %get-tuple-element.197) | copy-start | bytes 9220
  701.0 22.9 %copy-start.162 = (f32[768]{0:T(1024)S(1)}, f32[768]{0:T(1024)}, u32[]{:S(2)}) copy-start(f32[768]{0:T(1024)} %get-tuple-element.199) | copy-start | bytes 9220
  701.0 22.9 %copy-start.161 = (f32[768]{0:T(1024)S(1)}, f32[768]{0:T(1024)}, u32[]{:S(2)}) copy-start(f32[768]{0:T(1024)} %get-tuple-element.204) | copy-start | bytes 9220
  768.8 24.5 %slice-start.7 = ((s8[7077888]{0:T(1024)(128)(4,1)}), s8[2883584]{0:T(1024)(128)(4,1)S(1)}, s32[]{:S(2)}) async-start(s8[7077888]{0:T(1024)(128)(4,1)} %bitcast.363), calls=%async_computation.8 | async-start | bytes 5767168
  (166 other events, 855.0 us)
Sparse Core Ops, SparseCore 0:
  455.1 131.1 all-reduce.6
